TPU v7x, 32 devices: a whole 2x2x4 slice. The times are simulated.
32 devices in a mesh: rep: 8 (over y, x, core), shard: 4 (over z).
Axes of the slice: x: 2, y: 2, z: 4, core: 2. Of those that a mesh axis runs over, the one named last changes fastest.
Arguments:
- tokens: float32 [32768, 768], P(('rep', 'shard')), may hold values from -6 to 6
- cotangent: float32 [32768, 768], P(('rep', 'shard')), may hold values from -6 to 6
- lengths: int32 [32, 8], P(('rep', 'shard')), may hold values from 0 to 1024, as said below
- proj_weight: float32 [768, 3352], P('shard'), may hold values from -0.21875 to 0.21875
- proj_first: float32 [768, 3352], P('shard'), as said below
- proj_second: float32 [768, 3352], P('shard'), as said below
- out_weight: float32 [1536, 768], P('shard'), may hold values from -0.15625 to 0.15625
- out_first: float32 [1536, 768], P('shard'), as said below
- out_second: float32 [1536, 768], P('shard'), as said below
- small_params: float32 [11336], P('shard'), as said below
- small_first: float32 [11336], P('shard'), as said below
- small_second: float32 [11336], P('shard'), as said below
Outputs:
- block_out: float32 [32768, 768], P(('rep', 'shard'))
- token_grad: float32 [32768, 768], P(('rep', 'shard'))
- proj_new: float32 [768, 3352], P('shard')
- proj_first_new: float32 [768, 3352], P('shard')
- proj_second_new: float32 [768, 3352], P('shard')
- out_new: float32 [1536, 768], P('shard')
- out_first_new: float32 [1536, 768], P('shard')
- out_second_new: float32 [1536, 768], P('shard')
- small_new: float32 [11336], P('shard')
- small_first_new: float32 [11336], P('shard')
- small_second_new: float32 [11336], P('shard')
Inputs may be any that keep to these rules, and one draw needn't show every extreme that they name: Each row lists the lengths of the sequences of one pack, zeros allowed; a row sums to at most 1024 and to at least 256; in every draw some row holds one sequence of exactly 1024. `small_params`: gains within 0.6 to 1.4, convolution weights within -0.9 to 0.9, convolution bias within -0.5 to 0.5, step bias within -7 to -2.2, log decay rates within 0 to log 16, skip gains within 0.5 to 1.5. `proj_first`: both signs. `proj_second`: Positive. `out_first`: both signs. `out_second`: Positive. `small_first`: both signs. `small_second`: Positive.
All inputs are finite; a program needn't handle non-finite values.
Results may differ from a plain program's by a relative error of at most 0.012.
The roundings to bfloat16 on the way count: a program that leaves them out, or rounds other values in their place, can miss the bound.
Values may be sent and summed in bfloat16 or wider, within the bound.
A program may use at most 448 MiB of HBM per device.

v0:
```python
import jax
import jax.numpy as jnp
from jax import lax
from jax.sharding import PartitionSpec as P

D = 768
P_SIZE = 64
N = 128
K = 4
BLOCK = 256
STEP = 10
DI = 1536
H = 24
CH = 1792


EPS_NORM = 1e-05
BETA_ONE = 0.9
BETA_TWO = 0.95
ADAM_EPS = 1e-08
DECAY_WEIGHT = 0.1
RATE_PROJ = 0.03
RATE_OUT = 0.02
RATE_SMALL = 0.4
highest = lax.Precision.HIGHEST


def unpack(small):
    offset = 0
    pieces = []
    for extent in (D, K * CH, CH, H, H, H, DI):
        pieces.append(small[offset : offset + extent])
        offset = offset + extent
    return (
        pieces[0],
        pieces[1].reshape(K, CH),
        pieces[2],
        pieces[3],
        pieces[4],
        pieces[5],
        pieces[6],
    )


def segments(row_lengths, row_count):
    edges = jnp.cumsum(row_lengths)
    places = jnp.arange(row_count, dtype=jnp.int32)
    segment = jnp.sum((places[:, None] >= edges[None, :]).astype(jnp.int32), axis=1)
    live_rows = (places < edges[-1]).astype(jnp.float32)
    return (segment, live_rows)


def convolve(conv_in, conv_weight, conv_bias, segment):
    row_count = conv_in.shape[0]
    total_sum = conv_bias + conv_weight[K - 1] * conv_in
    for shift_by in range(1, K):
        shifted = jnp.concatenate(
            [jnp.zeros((shift_by, conv_in.shape[1]), jnp.float32), conv_in[: row_count - shift_by]],
            axis=0,
        )
        earlier = jnp.concatenate(
            [jnp.full((shift_by,), -1, jnp.int32), segment[: row_count - shift_by]], axis=0
        )
        same_seg = (earlier == segment).astype(jnp.float32)
        total_sum = total_sum + conv_weight[K - 1 - shift_by] * shifted * same_seg[:, None]
    return jax.nn.silu(total_sum)


def block_scan(values, key_b, query_c, step_size, decay_log, segment):
    row_count = values.shape[0]
    blocks = row_count // BLOCK
    places = jnp.arange(BLOCK)

    def one_block(carry_in, inputs):
        state_h, last_seg = carry_in
        vals_c, keys_c, query_blk, step_blk, decay_blk, seg_blk = inputs
        running = jnp.cumsum(decay_blk, axis=0)
        allowed = (places[None, :] <= places[:, None]) & (seg_blk[None, :] == seg_blk[:, None])
        run_t = running.T
        spread_log = run_t[:, :, None] - run_t[:, None, :]
        factor = jnp.where(allowed[None], jnp.exp(jnp.where(allowed[None], spread_log, 0.0)), 0.0)
        scores = jnp.dot(query_blk, keys_c.T, precision=highest)
        weights = factor * scores[None] * step_blk.T[:, None, :]
        inner_y = jnp.einsum("hts,shp->thp", weights, vals_c, precision=highest)
        carried = (seg_blk == last_seg).astype(jnp.float32)
        reach_in = jnp.exp(running) * carried[:, None]
        outer_y = (
            jnp.einsum("tn,hpn->thp", query_blk, state_h, precision=highest) * reach_in[:, :, None]
        )
        tail_seg = seg_blk[BLOCK - 1]
        keep_w = (
            jnp.exp(running[BLOCK - 1][None, :] - running)
            * step_blk
            * (seg_blk == tail_seg).astype(jnp.float32)[:, None]
        )
        fresh_st = jnp.einsum("shp,sn->hpn", keep_w[:, :, None] * vals_c, keys_c, precision=highest)
        stay_w = jnp.exp(running[BLOCK - 1]) * (tail_seg == last_seg).astype(jnp.float32)
        return ((fresh_st + stay_w[:, None, None] * state_h, tail_seg), inner_y + outer_y)

    inputs = (
        values.reshape(blocks, BLOCK, H, P_SIZE),
        key_b.reshape(blocks, BLOCK, N),
        query_c.reshape(blocks, BLOCK, N),
        step_size.reshape(blocks, BLOCK, H),
        decay_log.reshape(blocks, BLOCK, H),
        segment.reshape(blocks, BLOCK),
    )
    start_state = (jnp.zeros((H, P_SIZE, N), jnp.float32), jnp.array(-1, jnp.int32))
    outputs = lax.scan(one_block, start_state, inputs)[1]
    return outputs.reshape(row_count, H, P_SIZE)


def mixer(projected, conv_weight, conv_bias, step_bias, rate_log, skip_gain, gain_out, segment):
    gate_z = projected[:, :DI]
    conv_in = projected[:, DI : DI + CH]
    step_raw = projected[:, DI + CH :]
    active = convolve(conv_in, conv_weight, conv_bias, segment)
    row_count = active.shape[0]
    values = active[:, :DI].reshape(row_count, H, P_SIZE)
    key_b = active[:, DI : DI + N]
    query_c = active[:, DI + N :]
    step_size = jax.nn.softplus(step_raw + step_bias)
    decay_log = -step_size * jnp.exp(rate_log)
    output = (
        block_scan(values, key_b, query_c, step_size, decay_log, segment)
        + skip_gain[None, :, None] * values
    )
    output = output.reshape(row_count, DI)
    gated = output * jax.nn.silu(gate_z)
    inv_rms = lax.rsqrt(jnp.mean(gated * gated, axis=1, keepdims=True) + EPS_NORM)
    return gated * inv_rms * gain_out


def pre_norm(rows_in, gain_in):
    inv_rms = lax.rsqrt(jnp.mean(rows_in * rows_in, axis=1, keepdims=True) + EPS_NORM)
    return rows_in * inv_rms * gain_in


def adam(weight, first, second, grad_sum, step_rate, decay_on):
    first_new = BETA_ONE * first + (1.0 - BETA_ONE) * grad_sum
    second_new = BETA_TWO * second + (1.0 - BETA_TWO) * grad_sum * grad_sum
    first_hat = first_new / (1.0 - BETA_ONE**STEP)
    second_hat = second_new / (1.0 - BETA_TWO**STEP)
    weight_new = weight - step_rate * (
        first_hat / (jnp.sqrt(second_hat) + ADAM_EPS) + decay_on * weight
    )
    return (weight_new, first_new, second_new)


def shards(
    tokens,
    cotangent,
    lengths,
    proj_weight,
    proj_first,
    proj_second,
    out_weight,
    out_first,
    out_second,
    small_params,
    small_first,
    small_second,
):
    row_count = tokens.shape[0]
    segment, live_rows = segments(lengths[0], row_count)
    proj_full, out_full, small_full = (
        lax.all_gather(proj_weight.astype(jnp.bfloat16), "shard", axis=0, tiled=True),
        lax.all_gather(out_weight.astype(jnp.bfloat16), "shard", axis=0, tiled=True),
        lax.all_gather(small_params.astype(jnp.bfloat16), "shard", axis=0, tiled=True),
    )
    params = unpack(small_full.astype(jnp.float32))
    normed, norm_back = jax.vjp(pre_norm, tokens, params[0])
    normed_low = normed.astype(jnp.bfloat16)
    projected = jnp.dot(normed_low, proj_full, preferred_element_type=jnp.float32)

    def local_mixer(proj_in, conv_weight, conv_bias, step_bias, rate_log, skip_gain, gain_out):
        return mixer(
            proj_in, conv_weight, conv_bias, step_bias, rate_log, skip_gain, gain_out, segment
        )

    mixed, mixer_back = jax.vjp(
        local_mixer, projected, params[1], params[2], params[3], params[4], params[5], params[6]
    )
    mixed_low = mixed.astype(jnp.bfloat16)
    branch = jnp.dot(mixed_low, out_full, preferred_element_type=jnp.float32)
    block_out = tokens + live_rows[:, None] * branch
    back_grad = (live_rows[:, None] * cotangent).astype(jnp.bfloat16)
    proj_back, out_back = (
        lax.all_gather(proj_weight.astype(jnp.bfloat16), "shard", axis=0, tiled=True),
        lax.all_gather(out_weight.astype(jnp.bfloat16), "shard", axis=0, tiled=True),
    )
    out_grad = lax.dot_general(
        mixed_low, back_grad, (((0,), (0,)), ((), ())), preferred_element_type=jnp.float32
    )
    d_mixed = lax.dot_general(
        back_grad, out_back, (((1,), (1,)), ((), ())), preferred_element_type=jnp.float32
    )
    mixer_grads = mixer_back(d_mixed)
    d_projected = mixer_grads[0].astype(jnp.bfloat16)
    proj_grad = lax.dot_general(
        normed_low, d_projected, (((0,), (0,)), ((), ())), preferred_element_type=jnp.float32
    )
    d_normed = lax.dot_general(
        d_projected, proj_back, (((1,), (1,)), ((), ())), preferred_element_type=jnp.float32
    )
    d_rows, d_gain = norm_back(d_normed)
    token_grad = cotangent + d_rows
    small_grad = jnp.concatenate(
        [
            d_gain,
            mixer_grads[1].reshape(-1),
            mixer_grads[2],
            mixer_grads[3],
            mixer_grads[4],
            mixer_grads[5],
            mixer_grads[6],
        ]
    )
    whole_proj, whole_out, whole_small = lax.psum(
        (proj_grad, out_grad, small_grad), ("rep", "shard")
    )
    owner_idx = lax.axis_index("shard")
    sum_proj = lax.dynamic_slice_in_dim(
        whole_proj, owner_idx * proj_weight.shape[0], proj_weight.shape[0], 0
    )
    sum_out = lax.dynamic_slice_in_dim(
        whole_out, owner_idx * out_weight.shape[0], out_weight.shape[0], 0
    )
    sum_small = lax.dynamic_slice_in_dim(
        whole_small, owner_idx * small_params.shape[0], small_params.shape[0], 0
    )
    proj_new, proj_first_new, proj_second_new = adam(
        proj_weight, proj_first, proj_second, sum_proj, RATE_PROJ, DECAY_WEIGHT
    )
    out_new, out_first_new, out_second_new = adam(
        out_weight, out_first, out_second, sum_out, RATE_OUT, DECAY_WEIGHT
    )
    small_new, small_first_new, small_second_new = adam(
        small_params, small_first, small_second, sum_small, RATE_SMALL, 0.0
    )
    return (
        block_out,
        token_grad,
        proj_new,
        proj_first_new,
        proj_second_new,
        out_new,
        out_first_new,
        out_second_new,
        small_new,
        small_first_new,
        small_second_new,
    )


def solution(mesh):
    in_specs = (
        P(("rep", "shard"), None),
        P(("rep", "shard"), None),
        P(("rep", "shard"), None),
        P("shard", None),
        P("shard", None),
        P("shard", None),
        P("shard", None),
        P("shard", None),
        P("shard", None),
        P("shard"),
        P("shard"),
        P("shard"),
    )
    out_specs = (
        P(("rep", "shard"), None),
        P(("rep", "shard"), None),
        P("shard", None),
        P("shard", None),
        P("shard", None),
        P("shard", None),
        P("shard", None),
        P("shard", None),
        P("shard"),
        P("shard"),
        P("shard"),
    )
    return jax.shard_map(shards, mesh=mesh, in_specs=in_specs, out_specs=out_specs, check_vma=False)
```

profile of v0, /device:TPU:0, one launch (start us, length us, event | category | flops | bytes accessed | tf_op | source)
XLA Modules:
  0.0 1287.4 jit_solution(16254371969307429789)
XLA Ops:
  14.1 22.2 %all-reduce.20 = bf16[11336]{0:T(1024)(128)(2,1)S(1)} all-reduce(bf16[11336]{0:T(1024)(128)(2,1)S(1)} %dynamic-update-slice), channel_id=1, replica_groups=mesh['rep'=8,'shard'=4] {'shard'}, use_global_device_ids=true, to_apply=%add.20 | all-reduce | flops 11336 | bytes 45344
  40.7 72.0 %all-gather.3.cloned.1.call-done = bf16[768,3352]{1,0:T(8,128)(2,1)} async-done(((bf16[192,3352]{1,0:T(8,128)(2,1)}), bf16[768,3352]{1,0:T(8,128)(2,1)}) %all-gather.3.cloned.1.call-update) | async-done | bytes 5148688 | tf_op jit(solution)/shard_map/all_gather | solution.py:167
  112.7 9.5 fusion.165
  134.6 17.7 %fusion.142 = (f32[1024,1792]{0,1:T(8,128)}, f32[1024,1792]{0,1:T(8,128)}) fusion(f32[1024]{0:T(1024)S(1)} %get-tuple-element.1864, f32[1021,1792]{0,1:T(8,128)} %slice.174, f32[1792]{0:T(1024)S(1)} %get-tuple-element.1862, f32[1024]{0:T(1024)S(1)} %get-tuple-element.1865, f32[1022,1792]{0,1:T(8,128)} %slice.172, f32[1792]{0:T(1024)S(1)} %get-tuple-element.1861, ...), kind=kLoop, calls=%fused_computation.203 | loop fusion | flops 27525120 | bytes 44045312 | tf_op jit(solution)/shard_map/jvp(jit(silu))/mul | solution.py:66
  181.2 303.4 %while.85 = (s32[]{:T(128)}, f32[24,64,128]{2,1,0:T(8,128)S(1)}, s32[]{:T(128)}, f32[4,256,24,64]{1,0,3,2:T(4,128)}, pred[4,24,256,256]{3,2,1,0:T(32,128)(4,1)},...) while((s32[]{:T(128)}, f32[24,64,128]{2,1,0:T(8,128)S(1)}, ...), condition=%wide.region_6.7_spmd.clone, body=%wide.region_3.6_spmd.clone.sunk | while | flops 2535907328 | bytes 52454212 | solution.py:109
  185.5 9.4 multiply_dynamic-update-slice_fusion.4
  209.5 34.5 %dynamic_update_slice.295 = f32[4,256,24,64]{1,0,3,2:T(4,128)} dynamic-update-slice(f32[4,256,24,64]{1,0,3,2:T(4,128)} %get-tuple-element.2350, f32[1,256,24,64]{1,0,3,2:T(1,128)S(1)} %copy.284, s32[]{:T(128)} %get-tuple-element.2347, s32[]{:T(128)} %constant.245.clone.1..sunk, s32[]{:T(128)} %constant.245.clone.1..sunk, s32[]{:T(128)} %constant.245.clone.1..sunk) | dynamic-update-slice | bytes 3145732 | tf_op jit(solution)/shard_map/jvp()/while/body/jit(dynamic_update_index_in_dim)/dynamic_update_slice | solution.py:109
  261.3 9.4 multiply_dynamic-update-slice_fusion.4
  285.3 34.5 %dynamic_update_slice.295 = f32[4,256,24,64]{1,0,3,2:T(4,128)} dynamic-update-slice(f32[4,256,24,64]{1,0,3,2:T(4,128)} %get-tuple-element.2350, f32[1,256,24,64]{1,0,3,2:T(1,128)S(1)} %copy.284, s32[]{:T(128)} %get-tuple-element.2347, s32[]{:T(128)} %constant.245.clone.1..sunk, s32[]{:T(128)} %constant.245.clone.1..sunk, s32[]{:T(128)} %constant.245.clone.1..sunk) | dynamic-update-slice | bytes 3145732 | tf_op jit(solution)/shard_map/jvp()/while/body/jit(dynamic_update_index_in_dim)/dynamic_update_slice | solution.py:109
  337.2 9.5 multiply_dynamic-update-slice_fusion.4
  350.9 8.8 fusion.227
  361.3 34.5 %dynamic_update_slice.295 = f32[4,256,24,64]{1,0,3,2:T(4,128)} dynamic-update-slice(f32[4,256,24,64]{1,0,3,2:T(4,128)} %get-tuple-element.2350, f32[1,256,24,64]{1,0,3,2:T(1,128)S(1)} %copy.284, s32[]{:T(128)} %get-tuple-element.2347, s32[]{:T(128)} %constant.245.clone.1..sunk, s32[]{:T(128)} %constant.245.clone.1..sunk, s32[]{:T(128)} %constant.245.clone.1..sunk) | dynamic-update-slice | bytes 3145732 | tf_op jit(solution)/shard_map/jvp()/while/body/jit(dynamic_update_index_in_dim)/dynamic_update_slice | solution.py:109
  413.1 9.3 multiply_dynamic-update-slice_fusion.4
  426.7 8.8 fusion.227
  437.1 34.5 %dynamic_update_slice.295 = f32[4,256,24,64]{1,0,3,2:T(4,128)} dynamic-update-slice(f32[4,256,24,64]{1,0,3,2:T(4,128)} %get-tuple-element.2350, f32[1,256,24,64]{1,0,3,2:T(1,128)S(1)} %copy.284, s32[]{:T(128)} %get-tuple-element.2347, s32[]{:T(128)} %constant.245.clone.1..sunk, s32[]{:T(128)} %constant.245.clone.1..sunk, s32[]{:T(128)} %constant.245.clone.1..sunk) | dynamic-update-slice | bytes 3145732 | tf_op jit(solution)/shard_map/jvp()/while/body/jit(dynamic_update_index_in_dim)/dynamic_update_slice | solution.py:109
  513.7 13.3 %multiply_reduce_fusion.6 = (f32[1536]{0:T(1024)}, f32[1024,1536]{0,1:T(8,128)}, f32[1024,1536]{0,1:T(8,128)}) fusion(f32[1024,1792]{0,1:T(8,128)} %get-tuple-element.1822, f32[1024,3352]{0,1:T(8,128)} %copy-done.1, f32[1024,1536]{0,1:T(8,128)S(1)} %copy-done.6, f32[1024]{0:T(1024)S(1)} %multiply_multiply_fusion.4, f32[1024]{0:T(1024)S(1)} %fusion.160, ...), kind=kLoop, calls=%fused_computation.208 | loop fusion | flops 33028608 | bytes 44066816 | tf_op jit(solution)/shard_map/transpose(jvp())/reduce_sum | solution.py:126
  541.5 377.2 %while.86 = (s32[]{:T(128)}, f32[24,64,128]{2,1,0:T(8,128)S(1)}, f32[4,256,24,64]{1,0,3,2:T(4,128)}, f32[4,256,128]{2,1,0:T(8,128)}, f32[4,256,128]{2,1,0:T(8,12...) while((s32[]{:T(128)}, f32[24,64,128]{2,1,0:T(8,128)S(1)}, ...), condition=%wide.region_20.21_spmd.clone, body=%wide.region_9.20_spmd.clone.sunk | while | flops 5056032768 | bytes 64411468 | solution.py:109
  548.1 13.2 %fusion.246 = (f32[24,256]{1,0:T(8,128)S(1)}, f32[24,256]{1,0:T(8,128)S(1)}, f32[256,256]{1,0:T(8,128)S(1)}, f32[24,256]{1,0:T(8,128)S(1)}) fusion(f32[4,24,256,256]{3,2,1,0:T(8,128)} %get-tuple-element.2518, s32[]{:T(128)S(6)} %sub.222, f32[256,256]{1,0:T(8,128)S(1)} %dynamic-slice_bitcast_fusion.11, ...), kind=kOutput, calls=%fused_computation.187.clone.1 | convolution fusion | flops 1225177088 | bytes 24216576 | tf_op jit(solution)/shard_map/transpose(jvp())/while/body/eval_jaxpr/hts,shp->thp/dot_general | solution.py:84
  586.7 34.7 %dynamic_update_slice.300 = f32[4,256,24,64]{1,0,3,2:T(4,128)} dynamic-update-slice(f32[4,256,24,64]{1,0,3,2:T(4,128)} %get-tuple-element.2453, f32[1,256,24,64]{1,0,3,2:T(1,128)} %copy.292, s32[]{:T(128)S(6)} %sub.222, s32[]{:T(128)} %constant.245.clone.1..sunk.1, s32[]{:T(128)} %constant.245.clone.1..sunk.1, s32[]{:T(128)} %constant.245.clone.1..sunk.1) | dynamic-update-slice | bytes 3145732 | tf_op jit(solution)/shard_map/transpose(jvp())/while/body/jit(dynamic_update_index_in_dim)/dynamic_update_slice | solution.py:109
  642.2 13.2 %fusion.246 = (f32[24,256]{1,0:T(8,128)S(1)}, f32[24,256]{1,0:T(8,128)S(1)}, f32[256,256]{1,0:T(8,128)S(1)}, f32[24,256]{1,0:T(8,128)S(1)}) fusion(f32[4,24,256,256]{3,2,1,0:T(8,128)} %get-tuple-element.2518, s32[]{:T(128)S(6)} %sub.222, f32[256,256]{1,0:T(8,128)S(1)} %dynamic-slice_bitcast_fusion.11, ...), kind=kOutput, calls=%fused_computation.187.clone.1 | convolution fusion | flops 1225177088 | bytes 24216576 | tf_op jit(solution)/shard_map/transpose(jvp())/while/body/eval_jaxpr/hts,shp->thp/dot_general | solution.py:84
  680.9 34.7 %dynamic_update_slice.300 = f32[4,256,24,64]{1,0,3,2:T(4,128)} dynamic-update-slice(f32[4,256,24,64]{1,0,3,2:T(4,128)} %get-tuple-element.2453, f32[1,256,24,64]{1,0,3,2:T(1,128)} %copy.292, s32[]{:T(128)S(6)} %sub.222, s32[]{:T(128)} %constant.245.clone.1..sunk.1, s32[]{:T(128)} %constant.245.clone.1..sunk.1, s32[]{:T(128)} %constant.245.clone.1..sunk.1) | dynamic-update-slice | bytes 3145732 | tf_op jit(solution)/shard_map/transpose(jvp())/while/body/jit(dynamic_update_index_in_dim)/dynamic_update_slice | solution.py:109
  736.4 13.2 %fusion.246 = (f32[24,256]{1,0:T(8,128)S(1)}, f32[24,256]{1,0:T(8,128)S(1)}, f32[256,256]{1,0:T(8,128)S(1)}, f32[24,256]{1,0:T(8,128)S(1)}) fusion(f32[4,24,256,256]{3,2,1,0:T(8,128)} %get-tuple-element.2518, s32[]{:T(128)S(6)} %sub.222, f32[256,256]{1,0:T(8,128)S(1)} %dynamic-slice_bitcast_fusion.11, ...), kind=kOutput, calls=%fused_computation.187.clone.1 | convolution fusion | flops 1225177088 | bytes 24216576 | tf_op jit(solution)/shard_map/transpose(jvp())/while/body/eval_jaxpr/hts,shp->thp/dot_general | solution.py:84
  775.0 34.7 %dynamic_update_slice.300 = f32[4,256,24,64]{1,0,3,2:T(4,128)} dynamic-update-slice(f32[4,256,24,64]{1,0,3,2:T(4,128)} %get-tuple-element.2453, f32[1,256,24,64]{1,0,3,2:T(1,128)} %copy.292, s32[]{:T(128)S(6)} %sub.222, s32[]{:T(128)} %constant.245.clone.1..sunk.1, s32[]{:T(128)} %constant.245.clone.1..sunk.1, s32[]{:T(128)} %constant.245.clone.1..sunk.1) | dynamic-update-slice | bytes 3145732 | tf_op jit(solution)/shard_map/transpose(jvp())/while/body/jit(dynamic_update_index_in_dim)/dynamic_update_slice | solution.py:109
  830.6 13.2 %fusion.246 = (f32[24,256]{1,0:T(8,128)S(1)}, f32[24,256]{1,0:T(8,128)S(1)}, f32[256,256]{1,0:T(8,128)S(1)}, f32[24,256]{1,0:T(8,128)S(1)}) fusion(f32[4,24,256,256]{3,2,1,0:T(8,128)} %get-tuple-element.2518, s32[]{:T(128)S(6)} %sub.222, f32[256,256]{1,0:T(8,128)S(1)} %dynamic-slice_bitcast_fusion.11, ...), kind=kOutput, calls=%fused_computation.187.clone.1 | convolution fusion | flops 1225177088 | bytes 24216576 | tf_op jit(solution)/shard_map/transpose(jvp())/while/body/eval_jaxpr/hts,shp->thp/dot_general | solution.py:84
  869.2 34.7 %dynamic_update_slice.300 = f32[4,256,24,64]{1,0,3,2:T(4,128)} dynamic-update-slice(f32[4,256,24,64]{1,0,3,2:T(4,128)} %get-tuple-element.2453, f32[1,256,24,64]{1,0,3,2:T(1,128)} %copy.292, s32[]{:T(128)S(6)} %sub.222, s32[]{:T(128)} %constant.245.clone.1..sunk.1, s32[]{:T(128)} %constant.245.clone.1..sunk.1, s32[]{:T(128)} %constant.245.clone.1..sunk.1) | dynamic-update-slice | bytes 3145732 | tf_op jit(solution)/shard_map/transpose(jvp())/while/body/jit(dynamic_update_index_in_dim)/dynamic_update_slice | solution.py:109
  930.1 13.2 %multiply_reduce_fusion.4 = (f32[1792]{0:T(1024)S(1)}, f32[1024,1792]{0,1:T(8,128)}, f32[1024,1792]{0,1:T(8,128)}) fusion(f32[1021,1792]{0,1:T(8,128)} %slice.174, f32[1024]{0:T(1024)S(1)} %copy-done.35, f32[1024,1792]{0,1:T(8,128)} %get-tuple-element.1823, f32[1024,1536]{0,1:T(8,128)} %multiply_add_fusion.2, f32[1024,128]{0,1:T(8,128)S(1)} %copy.165, ...), kind=kLoop, calls=%fused_computation.200 | loop fusion | flops 25688320 | bytes 36689920 | tf_op jit(solution)/shard_map/transpose(jvp())/reduce_sum | solution.py:65
  943.4 12.1 multiply_reduce_fusion.3
  975.7 14.7 %fusion.167 = (f32[1792]{0:T(1024)S(1)}, f32[1792]{0:T(1024)S(1)}, f32[1024,1792]{0,1:T(8,128)}) fusion(f32[1024,1792]{0,1:T(8,128)S(1)} %bitcast.475, f32[1024,3352]{0,1:T(8,128)} %copy-done.1, f32[1792]{0:T(1024)S(1)} %copy-done.24, f32[1023,1792]{0,1:T(8,128)} %slice_multiply_fusion, f32[1022,1792]{0,1:T(8,128)} %slice_multiply_fusion.1, ...), kind=kLoop, calls=%fused_computation.275 | loop fusion | flops 12841472 | bytes 44018688 | tf_op jit(solution)/shard_map/transpose(jvp())/reduce_sum | solution.py:55
  990.5 15.0 %fusion.164 = f32[768,3352]{1,0:T(8,128)} fusion(f32[1024,768]{1,0:T(8,128)S(1)} %copy-done.7, f32[768]{0:T(1024)S(1)} %copy-done.40, f32[1024]{0:T(1024)S(1)} %copy-done.42, f32[1024,1536]{0,1:T(8,128)} %get-tuple-element.1849, f32[1024,1792]{0,1:T(8,128)} %get-tuple-element.1850, f32[1024,24]{0,1:T(8,128)S(1)} %get-tuple-element.1806), kind=kOutput, calls=%fused_computation.272 | convolution fusion | flops 5284896768 | bytes 27180032 | tf_op jit(solution)/shard_map/dot_general | solution.py:200
  1007.2 13.3 %multiply_reduce_fusion.9 = (f32[768]{0:T(1024)S(1)}, f32[1024]{0:T(1024)S(1)}, f32[1024,768]{1,0:T(8,128)}) fusion(f32[1024,768]{1,0:T(8,128)S(1)} %copy-done.7, f32[1024]{0:T(1024)S(1)} %copy-done.42, f32[768]{0:T(1024)S(1)} %copy-done.40, bf16[768,3352]{1,0:T(8,128)(2,1)} %all-gather.3.cloned.1.call-done, f32[1024,1536]{0,1:T(8,128)} %get-tuple-element.1849, ...), kind=kOutput, calls=%fused_computation.222 | convolution fusion | flops 5287254016 | bytes 25184256 | tf_op jit(solution)/shard_map/dot_general | solution.py:203
  1020.6 40.1 %psum.23 = f32[11336]{0:T(1024)S(1)} all-reduce(f32[11336]{0:T(1024)S(1)} %concatenate.31), channel_id=1, replica_groups=mesh['rep'=8,'shard'=4] {'rep','shard'}, use_global_device_ids=true, to_apply=%region_35.36 | all-reduce | flops 11336 | bytes 90688 | tf_op jit(solution)/shard_map/psum | solution.py:219
  1074.4 193.4 %all-reduce.24.cloned.1.call-done = (f32[768,3352]{1,0:T(8,128)}, f32[1536,768]{1,0:T(8,128)}) async-done(((f32[768,3352]{1,0:T(8,128)}, f32[1536,768]{1,0:T(8,128)}), (f32[768,3352]{1,0:T(8,128)}, f32[1536,768]{1,0:T(8,128)})) %all-reduce.24.cloned.1.call-update) | async-done | bytes 15015952 | tf_op jit(solution)/shard_map/psum | solution.py:219
  (470 shorter events, 443.7 us)
Async XLA Ops:
  7.2 29.5 %copy-start.55 = (s32[1,8]{1,0:T(1,128)S(1)}, s32[1,8]{1,0:T(1,128)}, u32[]{:S(2)}) copy-start(s32[1,8]{1,0:T(1,128)} %param.18) | copy-start | bytes 100
  7.2 105.5 %all-gather.3.cloned.1.call-start = ((), (), s32[]{:S(2)}) async-start(), calls=%async_computation | async-start | bytes 6635520 | tf_op jit(solution)/shard_map/all_gather | solution.py:167
  10.2 494.8 %all-gather.5.cloned.1.call-start = ((), (), s32[]{:S(2)}) async-start(), calls=%async_computation.1 | async-start | bytes 2949120 | tf_op jit(solution)/shard_map/all_gather | solution.py:168
  12.5 1255.4 %all-reduce.24.cloned.1.call-start = ((), (), s32[]{:S(2)}) async-start(), calls=%async_computation.2 | async-start | bytes 30670848 | tf_op jit(solution)/shard_map/psum | solution.py:219
  36.3 85.9 %copy-start.39 = (f32[768]{0:T(1024)}, f32[768]{0:T(1024)S(1)}, u32[]{:S(2)}) copy-start(f32[768]{0:T(1024)S(1)} %slice.162) | copy-start | bytes 9220
  36.3 98.2 %copy-start.17 = (f32[1792]{0:T(1024)}, f32[1792]{0:T(1024)S(1)}, u32[]{:S(2)}) copy-start(f32[1792]{0:T(1024)S(1)} %get-tuple-element.1862) | copy-start | bytes 21508
  36.3 98.2 %copy-start.19 = (f32[1792]{0:T(1024)}, f32[1792]{0:T(1024)S(1)}, u32[]{:S(2)}) copy-start(f32[1792]{0:T(1024)S(1)} %get-tuple-element.1860) | copy-start | bytes 21508
  36.3 98.2 %copy-start.21 = (f32[1792]{0:T(1024)}, f32[1792]{0:T(1024)S(1)}, u32[]{:S(2)}) copy-start(f32[1792]{0:T(1024)S(1)} %get-tuple-element.1861) | copy-start | bytes 21508
  36.3 98.2 %copy-start.23 = (f32[1792]{0:T(1024)}, f32[1792]{0:T(1024)S(1)}, u32[]{:S(2)}) copy-start(f32[1792]{0:T(1024)S(1)} %get-tuple-element.1859) | copy-start | bytes 21508
  36.4 85.9 %copy-start.25 = (f32[11336]{0:T(1024)}, f32[11336]{0:T(1024)S(1)}, u32[]{:S(2)}) copy-start(f32[11336]{0:T(1024)S(1)} %convert_element_type.110) | copy-start | bytes 136036
  36.7 477.0 %copy-start.36 = (f32[1536]{0:T(1024)}, f32[1536]{0:T(1024)S(1)}, u32[]{:S(2)}) copy-start(f32[1536]{0:T(1024)S(1)} %slice.180) | copy-start | bytes 18436
  39.7 82.5 %copy-start.32 = (f32[1024]{0:T(1024)}, f32[1024]{0:T(1024)S(1)}, u32[]{:S(2)}) copy-start(f32[1024]{0:T(1024)S(1)} %multiply_reduce_fusion.11) | copy-start | bytes 12292
  39.7 82.5 %copy-start.41 = (f32[1024]{0:T(1024)}, f32[1024]{0:T(1024)S(1)}, u32[]{:S(2)}) copy-start(f32[1024]{0:T(1024)S(1)} %fusion.159) | copy-start | bytes 12292
  39.8 136.2 %copy-start.48 = (f32[24]{0:T(128)}, f32[24]{0:T(128)S(1)}, u32[]{:S(2)}) copy-start(f32[24]{0:T(128)S(1)} %get-tuple-element.1857) | copy-start | bytes 292
  39.8 136.2 %copy-start.50 = (f32[24]{0:T(128)}, f32[24]{0:T(128)S(1)}, u32[]{:S(2)}) copy-start(f32[24]{0:T(128)S(1)} %get-tuple-element.1868) | copy-start | bytes 292
  40.6 464.4 %copy-start.52 = (f32[1024]{0:T(1024)}, f32[1024]{0:T(1024)S(1)}, u32[]{:S(2)}) copy-start(f32[1024]{0:T(1024)S(1)} %fusion.155) | copy-start | bytes 12292
  40.7 93.8 %copy-start.28 = (f32[1024]{0:T(1024)}, f32[1024]{0:T(1024)S(1)}, u32[]{:S(2)}) copy-start(f32[1024]{0:T(1024)S(1)} %get-tuple-element.1863) | copy-start | bytes 12292
  40.7 93.8 %copy-start.30 = (f32[1024]{0:T(1024)}, f32[1024]{0:T(1024)S(1)}, u32[]{:S(2)}) copy-start(f32[1024]{0:T(1024)S(1)} %get-tuple-element.1865) | copy-start | bytes 12292
  40.7 93.8 %copy-start.34 = (f32[1024]{0:T(1024)}, f32[1024]{0:T(1024)S(1)}, u32[]{:S(2)}) copy-start(f32[1024]{0:T(1024)S(1)} %get-tuple-element.1864) | copy-start | bytes 12292
  122.3 12.3 copy-start.1
  497.6 16.1 %copy-start.43 = (f32[1024]{0:T(1024)}, f32[1024]{0:T(1024)S(1)}, u32[]{:S(2)}) copy-start(f32[1024]{0:T(1024)S(1)} %fusion.160) | copy-start | bytes 12292
  930.1 13.2 %copy-start.29 = (f32[1024]{0:T(1024)S(1)}, f32[1024]{0:T(1024)}, u32[]{:S(2)}) copy-start(f32[1024]{0:T(1024)} %copy-done.28) | copy-start | bytes 12292
  930.1 13.2 %copy-start.31 = (f32[1024]{0:T(1024)S(1)}, f32[1024]{0:T(1024)}, u32[]{:S(2)}) copy-start(f32[1024]{0:T(1024)} %copy-done.30) | copy-start | bytes 12292
  960.7 14.9 %slice-start = ((s8[7340032]{0:T(1024)(128)(4,1)}), s8[4194304]{0:T(1024)(128)(4,1)S(1)}, s32[]{:S(2)}) async-start(s8[7340032]{0:T(1024)(128)(4,1)} %bitcast.474), calls=%async_computation.3 | async-start | bytes 8388608
  975.7 14.8 %copy-start.7 = (f32[1024,768]{1,0:T(8,128)S(1)}, f32[1024,768]{1,0:T(8,128)}, u32[]{:S(2)}) copy-start(f32[1024,768]{1,0:T(8,128)} %param.16) | copy-start | bytes 9437188
  975.7 14.8 %copy-start.40 = (f32[768]{0:T(1024)S(1)}, f32[768]{0:T(1024)}, u32[]{:S(2)}) copy-start(f32[768]{0:T(1024)} %copy-done.39) | copy-start | bytes 9220
  975.7 14.8 %copy-start.42 = (f32[1024]{0:T(1024)S(1)}, f32[1024]{0:T(1024)}, u32[]{:S(2)}) copy-start(f32[1024]{0:T(1024)} %copy-done.41) | copy-start | bytes 12292
  1007.1 13.4 %copy-start.47 = (f32[1536]{0:T(1024)S(1)}, f32[1536]{0:T(1024)}, u32[]{:S(2)}) copy-start(f32[1536]{0:T(1024)} %get-tuple-element.1662) | copy-start | bytes 18436
  1007.1 53.5 %copy-start.33 = (f32[1024]{0:T(1024)S(1)}, f32[1024]{0:T(1024)}, u32[]{:S(2)}) copy-start(f32[1024]{0:T(1024)} %copy-done.32) | copy-start | bytes 12292
  1007.1 53.6 %copy-start.27 = (f32[2834]{0:T(1024)S(1)}, f32[2834]{0:T(1024)}, u32[]{:S(2)}) copy-start(f32[2834]{0:T(1024)} %param.25) | copy-start | bytes 34012
  1007.1 53.6 %copy-start.45 = (f32[2834]{0:T(1024)S(1)}, f32[2834]{0:T(1024)}, u32[]{:S(2)}) copy-start(f32[2834]{0:T(1024)} %param.26) | copy-start | bytes 34012
  1007.1 53.6 %copy-start.46 = (f32[2834]{0:T(1024)S(1)}, f32[2834]{0:T(1024)}, u32[]{:S(2)}) copy-start(f32[2834]{0:T(1024)} %param.27) | copy-start | bytes 34012
  (30 other events, 212.0 us)
Sparse Core Ops, SparseCore 0:
  10.4 102.2 all-gather.2
  114.8 48.9 all-gather.4
  1005.6 262.1 all-reduce.23
where the time goes:
time: 1310 us; the launch traced here: 1290 us
  local copies, waits for them, and re-layouts  418 us (32%)
  matrix products  284 us (22%)
  waiting for transfers between devices  265 us (20%)
  other arithmetic  235 us (18%)
  blocking collectives  62.2 us (5%)
  between operations  15.9 us (1%)
    dynamic_update_slice x56, local copies, waits for them, and re-layouts, block_scan(): outputs = lax.scan(one_block, start_state, inputs)[1]  315 us
    psum x1, waiting for transfers between devices, shards(): lax.psum((proj_grad, out_grad, small_grad), ('rep', 'shard'))  193 us
    dot_general x12, matrix products, one_block(): inner_y = jnp.einsum('hts,shp->thp', weights, vals_c, precision=highest)  117 us
    all_gather x1, waiting for transfers between devices, shards(): lax.all_gather(proj_weight.astype(jnp.bfloat16), 'shard', axis=0, tiled=T...  72 us
    dynamic_update_slice x28, other arithmetic, block_scan(): outputs = lax.scan(one_block, start_state, inputs)[1]  60.7 us
    dot_general x12, matrix products, one_block(): jnp.einsum('shp,sn->hpn', keep_w[:, :, None] * vals_c, keys_c, precision=...  44.3 us
    psum x1, blocking collectives, shards(): lax.psum((proj_grad, out_grad, small_grad), ('rep', 'shard'))  40.1 us
    dot_general x12, matrix products, one_block(): jnp.einsum('tn,hpn->thp', query_blk, state_h, precision=highest)  39.2 us
  transfers between devices with their start and end apart: 3, of which 2 were waited for; matrix products, arithmetic and copies ran while one was open for 33% of the time, Pallas kernels for 0%

commit v1 on v0

v1 whole, which is shorter than its diff:
```python
import functools

import jax
import jax.numpy as jnp
from jax import lax
from jax.experimental import pallas as pl
from jax.experimental.pallas import tpu as pltpu
from jax.sharding import PartitionSpec as P

D = 768
P_SIZE = 64
N = 128
K = 4
STEP = 10
DI = 1536
H = 24
CH = 1792
PROJ = 3352
WIDE = 3456
LANES = 128
L = 128
PAIRS = H // 2
TAIL = 8
FAR = -1e30
VMEM_BYTES = 56 * 1024 * 1024

EPS_NORM = 1e-05
BETA_ONE = 0.9
BETA_TWO = 0.95
ADAM_EPS = 1e-08
DECAY_WEIGHT = 0.1
RATE_PROJ = 0.03
RATE_OUT = 0.02
RATE_SMALL = 0.4
highest = lax.Precision.HIGHEST
f32 = jnp.float32
bf16 = jnp.bfloat16

CARRIED, KEPT, SAME, LATER = 0, 1, 2, 5


def dot(a, b, contract=((1,), (0,))):
    return lax.dot_general(a, b, (contract, ((), ())), preferred_element_type=f32)


def split(x):
    high = x.astype(bf16)
    return high, (x - high.astype(f32)).astype(bf16)


def expand(x, heads):
    high, low = split(x)
    return dot(high, heads) + dot(low, heads)


def head_sums(x, heads):
    high, low = split(x)
    return dot(high, heads, ((1,), (1,))) + dot(low, heads, ((1,), (1,)))


def sigmoid(x):
    return 1.0 / (1.0 + jnp.exp(-x))


def softplus(x):
    return jnp.maximum(x, 0.0) + jnp.log1p(jnp.exp(-jnp.abs(x)))


def triangle(lower):
    rows = lax.broadcasted_iota(jnp.int32, (L, L), 0)
    cols = lax.broadcasted_iota(jnp.int32, (L, L), 1)
    return (cols <= rows if lower else cols >= rows).astype(f32)


def conv_pre(ext_ref, flags, conv_w, conv_b):
    pre = conv_b + conv_w[K - 1 : K] * ext_ref[TAIL : TAIL + L]
    for shift_by in range(1, K):
        same = flags[:, SAME + shift_by - 1 : SAME + shift_by]
        pre = pre + conv_w[K - 1 - shift_by : K - shift_by] * (
            ext_ref[TAIL - shift_by : TAIL - shift_by + L] * same
        )
    return pre


def decays(step_raw, flags, stay, step_bias, rate):
    step = softplus(step_raw + step_bias)
    decay_log = -step * rate
    running = jnp.dot(triangle(True), decay_log, precision=highest, preferred_element_type=f32)
    last = running[L - 1 : L]
    reach = jnp.exp(running) * flags[:, CARRIED : CARRIED + 1]
    keep = jnp.exp(last - running) * flags[:, KEPT : KEPT + 1]
    stay_w = jnp.exp(last) * stay
    return step, decay_log, running, reach, keep, stay_w


def far_mask(seg_col, seg_row):
    rows = lax.broadcasted_iota(jnp.int32, (L, L), 0)
    cols = lax.broadcasted_iota(jnp.int32, (L, L), 1)
    return jnp.where((cols <= rows) & (seg_col == seg_row), 0.0, FAR)


def halves(pair):
    left = lax.broadcasted_iota(jnp.int32, pair.shape, 1) < P_SIZE
    zero = jnp.zeros_like(pair)
    return jnp.concatenate([jnp.where(left, pair, zero), jnp.where(left, zero, pair)], axis=0)


def forward_kernel(
    proj_ref, flags_ref, segc_ref, segr_ref, stay_ref, conv_w_ref, conv_b_ref, step_b_ref,
    rate_ref, skip_ref, gain_ref, heads_ref,
    mixed_ref, y_ref, states_ref, tails_ref,
    ext_ref, state_ref,
):
    @pl.when(pl.program_id(0) == 0)
    def _():
        ext_ref[L : L + TAIL] = jnp.zeros((TAIL, CH), f32)
        state_ref[...] = jnp.zeros((N, DI), f32)

    flags = flags_ref[...]
    heads = heads_ref[...]
    tail = ext_ref[L : L + TAIL]
    ext_ref[0:TAIL] = tail
    tails_ref[...] = tail
    ext_ref[TAIL : TAIL + L] = proj_ref[:, DI : DI + CH]
    pre = conv_pre(ext_ref, flags, conv_w_ref[...], conv_b_ref[...])
    active = pre * sigmoid(pre)
    values = active[:, :DI]
    keys = active[:, DI : DI + N].astype(bf16)
    query = active[:, DI + N :].astype(bf16)
    step, _, running, reach, keep, stay_w = decays(
        proj_ref[:, DI + CH :], flags, stay_ref[0], step_b_ref[...], rate_ref[...]
    )
    run_t = running.T
    far = far_mask(segc_ref[...], segr_ref[0])
    scores = dot(query, keys, ((1,), (1,)))
    scaled = (values * expand(step, heads)).astype(bf16)
    state = state_ref[...]
    states_ref[0] = state
    outer = dot(query, state.astype(bf16)) * expand(reach, heads)
    inner = []
    for pair in range(PAIRS):
        weights = []
        for h in (2 * pair, 2 * pair + 1):
            factor = jnp.exp(running[:, h : h + 1] - run_t[h : h + 1, :] + far)
            weights.append((factor * scores).astype(bf16))
        stacked = halves(scaled[:, pair * LANES : (pair + 1) * LANES])
        inner.append(dot(jnp.concatenate(weights, axis=1), stacked))
    y = jnp.concatenate(inner, axis=1) + outer + skip_ref[...] * values
    y_ref[...] = y
    fresh = (values * expand(keep * step, heads)).astype(bf16)
    state_ref[...] = state * expand(jnp.broadcast_to(stay_w, (8, LANES)), heads)[0:1] + dot(
        keys, fresh, ((0,), (0,))
    )
    gate = proj_ref[:, :DI]
    gated = y * (gate * sigmoid(gate))
    inv_rms = lax.rsqrt(jnp.mean(gated * gated, axis=1, keepdims=True) + EPS_NORM)
    mixed_ref[...] = (gated * inv_rms * gain_ref[...]).astype(bf16)


def backward_kernel(
    proj_ref, dmix_ref, y_ref, states_ref, tails_ref, flags_ref, segc_ref, segr_ref, stay_ref,
    conv_w_ref, conv_b_ref, step_b_ref, rate_ref, skip_ref, gain_ref, heads_ref,
    dproj_ref, gconv_ref, ghead_ref, gwide_ref,
    ext_ref, dext_ref, dstate_ref, cross_ref,
):
    @pl.when(pl.program_id(0) == 0)
    def _():
        dext_ref[0:TAIL] = jnp.zeros((TAIL, CH), f32)
        dstate_ref[...] = jnp.zeros((N, DI), f32)
        cross_ref[...] = jnp.zeros((8, LANES), f32)
        gconv_ref[...] = jnp.zeros((8, CH), f32)
        ghead_ref[...] = jnp.zeros((8, LANES), f32)
        gwide_ref[...] = jnp.zeros((8, DI), f32)

    flags = flags_ref[...]
    heads = heads_ref[...]
    skip = skip_ref[...]
    rate = rate_ref[...]
    ext_ref[0:TAIL] = tails_ref[...]
    ext_ref[TAIL : TAIL + L] = proj_ref[:, DI : DI + CH]
    pre = conv_pre(ext_ref, flags, conv_w_ref[...], conv_b_ref[...])
    sig = sigmoid(pre)
    active = pre * sig
    values = active[:, :DI]
    keys = active[:, DI : DI + N].astype(bf16)
    query = active[:, DI + N :].astype(bf16)
    step_in = proj_ref[:, DI + CH :]
    step, decay_log, running, reach, keep, stay_w = decays(
        step_in, flags, stay_ref[0], step_b_ref[...], rate
    )

    gate = proj_ref[:, :DI]
    y = y_ref[...]
    dmix = dmix_ref[...]
    gate_sig = sigmoid(gate)
    silu = gate * gate_sig
    gated = y * silu
    inv_rms = lax.rsqrt(jnp.mean(gated * gated, axis=1, keepdims=True) + EPS_NORM)
    gwide_ref[0:1] += jnp.sum(dmix * (gated * inv_rms), axis=0, keepdims=True)
    q = dmix * gain_ref[...]
    slope = inv_rms * inv_rms * inv_rms * jnp.mean(q * gated, axis=1, keepdims=True)
    dgated = inv_rms * q - gated * slope
    dy = dgated * silu
    dproj_ref[:, :DI] = (dgated * y * (gate_sig * (1.0 + gate * (1.0 - gate_sig)))).astype(bf16)
    gwide_ref[1:2] += jnp.sum(dy * values, axis=0, keepdims=True)

    run_t = running.T
    far = far_mask(segc_ref[...], segr_ref[0])
    scores = dot(query, keys, ((1,), (1,)))
    step_wide = expand(step, heads)
    scaled = (values * step_wide).astype(bf16)
    dy_low = dy.astype(bf16)
    lane = lax.broadcasted_iota(jnp.int32, (L, LANES), 1)
    left = lane < P_SIZE
    f_sum = jnp.zeros((L, L), f32)
    row_sums = jnp.zeros((L, LANES), f32)
    col_sums = []
    inner = []
    for pair in range(PAIRS):
        columns = slice(pair * LANES, (pair + 1) * LANES)
        dy_pair = dy_low[:, columns]
        grads = dot(dy_pair, halves(scaled[:, columns]), ((1,), (1,)))
        weights = []
        for half in range(2):
            h = 2 * pair + half
            factor = jnp.exp(running[:, h : h + 1] - run_t[h : h + 1, :] + far)
            weight = factor * scores
            grad = grads[:, half * L : (half + 1) * L]
            f_sum = f_sum + grad * factor
            e = grad * weight
            row_sums = jnp.where(lane == h, jnp.sum(e, axis=1, keepdims=True), row_sums)
            col_sums.append(jnp.sum(e, axis=0, keepdims=True))
            weights.append(weight.astype(bf16))
        both = dot(jnp.concatenate(weights, axis=1), dy_pair, ((0,), (0,)))
        inner.append(jnp.where(left, both[:L], both[L:]))
    col_sums.append(jnp.zeros((LANES - H, L), f32))
    col_sum = jnp.concatenate(col_sums, axis=0).T
    f_low = f_sum.astype(bf16)

    state = states_ref[0]
    state_low = state.astype(bf16)
    dstate = dstate_ref[...]
    dstate_low = dstate.astype(bf16)
    reach_wide = expand(reach, heads)
    keep_wide = expand(keep, heads)
    dy_reach = dy * reach_wide
    dy_reach_low = dy_reach.astype(bf16)
    row_in = head_sums(dy_reach * dot(query, state_low), heads)
    u_out = dot(keys, dstate_low) * keep_wide
    u_all = jnp.concatenate(inner, axis=1) + u_out
    fresh = (values * (keep_wide * step_wide)).astype(bf16)
    dquery = dot(f_low, keys) + dot(dy_reach_low, state_low, ((1,), (1,)))
    dkeys = dot(f_low, query, ((0,), (0,))) + dot(fresh, dstate_low, ((1,), (1,)))
    dvalues = u_all * step_wide + skip * dy
    out_sum = head_sums(values * u_out, heads)
    dstep_own = head_sums(values * u_all, heads)
    drunning = row_sums - col_sum + row_in - step * out_sum
    ddecay = cross_ref[0:1] + jnp.dot(
        triangle(False), drunning, precision=highest, preferred_element_type=f32
    )
    dstate_new = dot(query, dy_reach_low, ((0,), (0,))) + dstate * expand(
        jnp.broadcast_to(stay_w, (8, LANES)), heads
    )[0:1]
    dstate_ref[...] = dstate_new
    cross_ref[...] = head_sums(
        jnp.broadcast_to(jnp.sum(dstate_new * state, axis=0, keepdims=True), (8, DI)), heads
    )
    dstep_raw = (dstep_own - rate * ddecay) * sigmoid(step_in + step_b_ref[...])
    ghead_ref[0:1] += jnp.sum(dstep_raw, axis=0, keepdims=True)
    ghead_ref[1:2] += jnp.sum(ddecay * decay_log, axis=0, keepdims=True)
    dproj_ref[:, DI + CH :] = dstep_raw.astype(bf16)

    dactive = jnp.concatenate([dvalues, dkeys, dquery], axis=1)
    dpre = dactive * (sig * (1.0 + pre * (1.0 - sig)))
    dext_ref[L : L + TAIL] = dext_ref[0:TAIL]
    dext_ref[0:L] = dpre
    conv_w = conv_w_ref[...]
    dconv = conv_w[K - 1 : K] * dpre
    gconv_ref[K : K + 1] += jnp.sum(dpre, axis=0, keepdims=True)
    gconv_ref[K - 1 : K] += jnp.sum(dpre * ext_ref[TAIL : TAIL + L], axis=0, keepdims=True)
    for shift_by in range(1, K):
        tap = K - 1 - shift_by
        same = flags[:, SAME + shift_by - 1 : SAME + shift_by]
        later = flags[:, LATER + shift_by - 1 : LATER + shift_by]
        dconv = dconv + conv_w[tap : tap + 1] * (dext_ref[shift_by : shift_by + L] * later)
        gconv_ref[tap : tap + 1] += jnp.sum(
            dpre * (ext_ref[TAIL - shift_by : TAIL - shift_by + L] * same), axis=0, keepdims=True
        )
    dproj_ref[:, DI : DI + CH] = dconv.astype(bf16)


def whole(shape):
    return pl.BlockSpec(shape, lambda i: (0,) * len(shape))


def run_forward(projected, marks, consts):
    rows = projected.shape[0]
    blocks = rows // L
    row = lambda i: (i, 0)
    deep = lambda i: (i, 0, 0)
    return pl.pallas_call(
        forward_kernel,
        grid=(blocks,),
        in_specs=[
            pl.BlockSpec((L, WIDE), row),
            pl.BlockSpec((L, 8), row),
            pl.BlockSpec((L, 1), row),
            pl.BlockSpec((1, 1, L), deep),
            pl.BlockSpec((1, 1, LANES), deep),
        ]
        + [whole(c.shape) for c in consts],
        out_specs=[
            pl.BlockSpec((L, DI), row),
            pl.BlockSpec((L, DI), row),
            pl.BlockSpec((1, N, DI), deep),
            pl.BlockSpec((TAIL, CH), row),
        ],
        out_shape=[
            jax.ShapeDtypeStruct((rows, DI), bf16),
            jax.ShapeDtypeStruct((rows, DI), f32),
            jax.ShapeDtypeStruct((blocks, N, DI), f32),
            jax.ShapeDtypeStruct((blocks * TAIL, CH), f32),
        ],
        scratch_shapes=[pltpu.VMEM((L + TAIL, CH), f32), pltpu.VMEM((N, DI), f32)],
        compiler_params=pltpu.CompilerParams(vmem_limit_bytes=VMEM_BYTES),
        name="mixer_forward",
    )(projected, *marks, *consts)


def run_backward(projected, dmix, y, states, tails, marks, consts):
    rows = projected.shape[0]
    blocks = rows // L
    row = lambda i: (blocks - 1 - i, 0)
    deep = lambda i: (blocks - 1 - i, 0, 0)
    return pl.pallas_call(
        backward_kernel,
        grid=(blocks,),
        in_specs=[
            pl.BlockSpec((L, WIDE), row),
            pl.BlockSpec((L, DI), row),
            pl.BlockSpec((L, DI), row),
            pl.BlockSpec((1, N, DI), deep),
            pl.BlockSpec((TAIL, CH), row),
            pl.BlockSpec((L, 8), row),
            pl.BlockSpec((L, 1), row),
            pl.BlockSpec((1, 1, L), deep),
            pl.BlockSpec((1, 1, LANES), deep),
        ]
        + [whole(c.shape) for c in consts],
        out_specs=[
            pl.BlockSpec((L, WIDE), row),
            whole((8, CH)),
            whole((8, LANES)),
            whole((8, DI)),
        ],
        out_shape=[
            jax.ShapeDtypeStruct((rows, WIDE), bf16),
            jax.ShapeDtypeStruct((8, CH), f32),
            jax.ShapeDtypeStruct((8, LANES), f32),
            jax.ShapeDtypeStruct((8, DI), f32),
        ],
        scratch_shapes=[
            pltpu.VMEM((L + TAIL, CH), f32),
            pltpu.VMEM((L + TAIL, CH), f32),
            pltpu.VMEM((N, DI), f32),
            pltpu.VMEM((8, LANES), f32),
        ],
        compiler_params=pltpu.CompilerParams(vmem_limit_bytes=VMEM_BYTES),
        name="mixer_backward",
    )(projected, dmix, y, states, tails, *marks, *consts)


def unpack(small):
    offset = 0
    pieces = []
    for extent in (D, K * CH, CH, H, H, H, DI):
        pieces.append(small[offset : offset + extent])
        offset = offset + extent
    return (
        pieces[0],
        pieces[1].reshape(K, CH),
        pieces[2],
        pieces[3],
        pieces[4],
        pieces[5],
        pieces[6],
    )


def row_marks(row_lengths, rows):
    edges = jnp.cumsum(row_lengths)
    blocks = rows // L

    def segment_at(places):
        inside = jnp.sum((places[:, None] >= edges[None, :]).astype(jnp.int32), axis=1)
        return jnp.where((places >= 0) & (places < rows), inside, -1)

    places = jnp.arange(rows, dtype=jnp.int32)
    starts = places - places % L
    segment = segment_at(places)
    before = segment_at(starts - 1)
    tail = segment_at(starts + L - 1)
    columns = [before, tail]
    columns += [segment_at(places - j) for j in range(1, K)]
    columns += [segment_at(places + j) for j in range(1, K)]
    flags = jnp.stack([(c == segment).astype(f32) for c in columns], axis=1)
    stay = (before == tail).astype(f32)[::L]
    marks = (
        flags,
        segment[:, None],
        segment.reshape(blocks, 1, L),
        jnp.broadcast_to(stay[:, None, None], (blocks, 1, LANES)),
    )
    live_rows = (places < edges[-1]).astype(f32)
    return marks, live_rows


def lanes(vector):
    return jnp.pad(vector, (0, LANES - H))[None]


def pre_norm(rows_in, gain_in):
    inv_rms = lax.rsqrt(jnp.mean(rows_in * rows_in, axis=1, keepdims=True) + EPS_NORM)
    return rows_in * inv_rms * gain_in


def adam(weight, first, second, grad_sum, step_rate, decay_on):
    first_new = BETA_ONE * first + (1.0 - BETA_ONE) * grad_sum
    second_new = BETA_TWO * second + (1.0 - BETA_TWO) * grad_sum * grad_sum
    first_hat = first_new / (1.0 - BETA_ONE**STEP)
    second_hat = second_new / (1.0 - BETA_TWO**STEP)
    weight_new = weight - step_rate * (
        first_hat / (jnp.sqrt(second_hat) + ADAM_EPS) + decay_on * weight
    )
    return (weight_new, first_new, second_new)


def total(grad):
    part = lax.psum_scatter(grad, ("shard", "rep"), scatter_dimension=0, tiled=True)
    return lax.all_gather(part, "rep", axis=0, tiled=True)


def gather(block):
    share = block.shape[0] // lax.axis_size("rep")
    own = lax.dynamic_slice_in_dim(block, lax.axis_index("rep") * share, share, 0)
    return lax.all_gather(own, ("shard", "rep"), axis=0, tiled=True)


def shards(
    tokens,
    cotangent,
    lengths,
    proj_weight,
    proj_first,
    proj_second,
    out_weight,
    out_first,
    out_second,
    small_params,
    small_first,
    small_second,
):
    rows = tokens.shape[0]
    marks, live_rows = row_marks(lengths[0], rows)
    block_rows, small_count = proj_weight.shape[0], small_params.shape[0]
    spare = block_rows * (WIDE - PROJ)
    riding = jnp.pad(small_params, (0, spare - small_count)).reshape(block_rows, WIDE - PROJ)
    proj_full = gather(jnp.concatenate([proj_weight, riding], axis=1).astype(bf16))
    out_full = gather(out_weight.astype(bf16))
    small_full = proj_full[:, PROJ:].reshape(-1, spare)[:, :small_count].reshape(-1)
    gain_in, conv_w, conv_b, step_b, rate_log, skip, gain_out = unpack(small_full.astype(f32))
    heads = jnp.pad(jnp.repeat(jnp.eye(H, dtype=bf16), P_SIZE, axis=1), ((0, LANES - H), (0, 0)))
    consts = (
        conv_w,
        conv_b[None],
        lanes(step_b),
        lanes(jnp.exp(rate_log)),
        jnp.repeat(skip, P_SIZE)[None],
        gain_out[None],
        heads,
    )
    normed, norm_back = jax.vjp(pre_norm, tokens, gain_in)
    normed_low = normed.astype(bf16)
    projected = dot(normed_low, proj_full)
    mixed_low, y, states, tails = run_forward(projected, marks, consts)
    back_grad = (live_rows[:, None] * cotangent).astype(bf16)
    out_grad = dot(mixed_low, back_grad, ((0,), (0,)))
    sum_out = total(out_grad)
    d_mixed = dot(back_grad, out_full, ((1,), (1,)))
    d_projected, gconv, ghead, gwide = run_backward(
        projected, d_mixed, y, states, tails, marks, consts
    )
    proj_grad = dot(normed_low, d_projected, ((0,), (0,)))
    sum_proj = total(proj_grad)[:, :PROJ]
    d_normed = dot(d_projected, proj_full, ((1,), (1,)))
    d_rows, d_gain = norm_back(d_normed)
    token_grad = cotangent + d_rows
    branch = dot(mixed_low, out_full)
    block_out = tokens + live_rows[:, None] * branch
    small_grad = jnp.concatenate(
        [
            d_gain,
            gconv[:K].reshape(-1),
            gconv[K],
            ghead[0, :H],
            ghead[1, :H],
            gwide[1].reshape(H, P_SIZE).sum(axis=1),
            gwide[0],
        ]
    )
    small_all = lax.psum(jnp.pad(small_grad, (0, -small_grad.shape[0] % 1024)).reshape(-1, LANES), ("rep", "shard"))
    sum_small = lax.dynamic_slice_in_dim(
        small_all.reshape(-1), lax.axis_index("shard") * small_count, small_count, 0
    )
    return (
        (block_out, token_grad)
        + adam(proj_weight, proj_first, proj_second, sum_proj, RATE_PROJ, DECAY_WEIGHT)
        + adam(out_weight, out_first, out_second, sum_out, RATE_OUT, DECAY_WEIGHT)
        + adam(small_params, small_first, small_second, sum_small, RATE_SMALL, 0.0)
    )


def solution(mesh):
    in_specs = (
        P(("rep", "shard"), None),
        P(("rep", "shard"), None),
        P(("rep", "shard"), None),
        P("shard", None),
        P("shard", None),
        P("shard", None),
        P("shard", None),
        P("shard", None),
        P("shard", None),
        P("shard"),
        P("shard"),
        P("shard"),
    )
    out_specs = (
        P(("rep", "shard"), None),
        P(("rep", "shard"), None),
        P("shard", None),
        P("shard", None),
        P("shard", None),
        P("shard", None),
        P("shard", None),
        P("shard", None),
        P("shard"),
        P("shard"),
        P("shard"),
    )
    return jax.shard_map(shards, mesh=mesh, in_specs=in_specs, out_specs=out_specs, check_vma=False)
```

time: 1310 us -> 482 us (0.37); the launches traced: 1290 us -> 481 us
  local copies, waits for them, and re-layouts: 418 us -> 24.7 us
  matrix products: 284 us -> 53.5 us
  other arithmetic: 235 us -> 30.4 us
  Pallas kernels: 0 us -> 76.9 us
  waiting for transfers between devices: 265 us -> 240 us
  blocking collectives: 62.2 us -> 40.3 us
    dynamic_update_slice x56 -> x0, local copies, waits for them, and re-layouts: 315 us -> none  [block_scan(): outputs = lax.scan(one_block, start_state, inputs)[1]]
    dot_general x54 -> x6, matrix products: 284 us -> 53.5 us  [dot(): lax.dot_general(a, b, (contract, ((), ())), preferred_element_type=f32)]
    psum x1 -> x0, waiting for transfers between devices: 193 us -> none  [shards(): lax.psum((proj_grad, out_grad, small_grad), ('rep', 'shard'))]
    unnamed x3 -> x7, waiting for transfers between devices: 0.05 us -> 148 us
    reduce_sum x20 -> x2, other arithmetic: 79.1 us -> 0.27 us  [the longest x1 0.16 us: segment_at(): jnp.sum((places[:, None] >= edges[None, :]).astype(jnp.int32), axis=1)]
    pallas_call x0 -> x2, Pallas kernels: none -> 76.9 us  [the longest x1 55.7 us: run_backward(): pl.pallas_call(backward_kernel, grid=(blocks,), in_specs=[pl.BlockSpec((L...]
    dynamic_update_slice x28 -> x0, other arithmetic: 60.7 us -> none  [block_scan(): outputs = lax.scan(one_block, start_state, inputs)[1]]
    mul x26 -> x0, other arithmetic: 42.4 us -> none  [the longest x3 18.9 us: convolve(): conv_weight[K - 1 - shift_by] * shifted * same_seg[:, None]]
  transfers between devices with their start and end apart: 3 -> 6, of which waited for: 2 -> 4; matrix products, arithmetic and copies ran while one was open for 33% -> 20% of each run, Pallas kernels for 0% -> 16%
where the time goes in v1:
time: 482 us; the launch traced here: 481 us
  waiting for transfers between devices  240 us (50%)
  Pallas kernels  76.9 us (16%)
  matrix products  53.5 us (11%)
  blocking collectives  40.3 us (8%)
  other arithmetic  30.4 us (6%)
  local copies, waits for them, and re-layouts  24.7 us (5%)
  between operations  14.4 us (3%)
    unnamed x7, waiting for transfers between devices  148 us
    all_gather x2, waiting for transfers between devices, gather(): return lax.all_gather(own, ('shard', 'rep'), axis=0, tiled=True)  56.4 us
    pallas_call x1, Pallas kernels, run_backward(): pl.pallas_call(backward_kernel, grid=(blocks,), in_specs=[pl.BlockSpec((L...  55.7 us
    dot_general x6, matrix products, dot(): lax.dot_general(a, b, (contract, ((), ())), preferred_element_type=f32)  53.5 us
    psum x1, blocking collectives, shards(): lax.psum(jnp.pad(small_grad, (0, -small_grad.shape[0] % 1024)).reshape(-1...  40.3 us
    reduce_scatter x1, waiting for transfers between devices, total(): lax.psum_scatter(grad, ('shard', 'rep'), scatter_dimension=0, tiled=True)  35.9 us
    pallas_call x1, Pallas kernels, run_forward(): pl.pallas_call(forward_kernel, grid=(blocks,), in_specs=[pl.BlockSpec((L,...  21.3 us
    sub x3, other arithmetic, adam(): weight - step_rate * (first_hat / (jnp.sqrt(second_hat) + ADAM_EPS) + dec...  13.4 us
  transfers between devices with their start and end apart: 6, of which 4 were waited for; matrix products, arithmetic and copies ran while one was open for 20% of the time, Pallas kernels for 16%

profile of v1, /device:TPU:0, one launch (start us, length us, event | category | flops | bytes accessed | tf_op | source)
XLA Modules:
  0.0 480.9 jit_solution(2593401568250905636)
XLA Ops:
  8.1 1.9 convert.12
  10.8 1.5 dynamic-slice_convert_fusion
  13.5 1.0 copy.53
  14.5 1.0 copy.58
  15.5 1.0 copy.51
  16.5 1.0 copy.54
  17.6 1.0 copy.55
  18.6 1.0 copy.56
  19.6 1.0 copy.57
  20.7 1.0 copy.50
  21.7 1.0 copy.52
  22.7 4.0 select_compare_fusion
  28.3 1.7 pad.23.heads_ref
  30.0 3.2 stack.4
  36.4 42.8 %all-gather.5.cloned.1.call-done = bf16[768,3456]{1,0:T(8,128)(2,1)} async-done(((bf16[24,3456]{1,0:T(8,128)(2,1)}), bf16[768,3456]{1,0:T(8,128)(2,1)}) %all-gather.5.cloned.1.call-update) | async-done | bytes 5308432 | tf_op jit(solution)/shard_map/all_gather | solution.py:446
  79.2 1.0 slice.77
  84.0 11.7 %fusion.46.proj_ref = f32[1024,3456]{1,0:T(8,128)} fusion(bf16[768,3456]{1,0:T(8,128)(2,1)} %all-gather.5.cloned.1.call-done, f32[1024,768]{1,0:T(8,128)S(1)} %copy-done, f32[768]{0:T(1024)S(1)} %slice.79, f32[1024]{0:T(1024)S(1)} %fusion.42), kind=kOutput, calls=%fused_computation.117 | convolution fusion | flops 5438177280 | bytes 22617088 | tf_op jit(solution)/shard_map/dot_general | solution.py:43
  96.4 21.3 %mixer_forward.1 = (bf16[1024,1536]{1,0:T(8,128)(2,1)}, f32[1024,1536]{1,0:T(8,128)}, f32[8,128,1536]{2,1,0:T(8,128)}, f32[64,1792]{1,0:T(8,128)}) custom-call(f32[1024,3456]{1,0:T(8,128)} %fusion.46.proj_ref, f32[1024,8]{1,0:T(8,128)} %stack.5.flags_ref, s32[1024,1]{1,0:T(8,128)} %fusion.25.segc_ref, s32[8,1,128]{2,1,0:T(1,128)} %compare_select_fusion.segr_ref, ...), custom_call_target="tpu_custom_call" | custom-call | tf_op jit(solution)/shard_map/mixer_forward/pallas_call | solution.py:301
  117.7 6.8 %fusion.43 = f32[1536,768]{1,0:T(8,128)} fusion(bf16[1024,1536]{1,0:T(8,128)(2,1)} %get-tuple-element.19, f32[1024,768]{1,0:T(8,128)S(1)} %copy-done.3, f32[1024]{0:T(1024)S(1)} %fusion.40), kind=kOutput, calls=%fused_computation.114 | convolution fusion | flops 2417491968 | bytes 11014144 | tf_op jit(solution)/shard_map/dot_general | solution.py:43
  124.7 13.6 %all-gather.7.cloned.1.call-done = bf16[1536,768]{1,0:T(8,128)(2,1)} async-done(((bf16[48,768]{1,0:T(8,128)(2,1)}), bf16[1536,768]{1,0:T(8,128)(2,1)}) %all-gather.7.cloned.1.call-update) | async-done | bytes 2359312 | tf_op jit(solution)/shard_map/all_gather | solution.py:446
  138.3 7.9 %fusion.44.dmix_ref = f32[1024,1536]{1,0:T(8,128)} fusion(bf16[1536,768]{1,0:T(8,128)(2,1)} %all-gather.7.cloned.1.call-done, f32[1024,768]{1,0:T(8,128)} %param.13, f32[1024]{0:T(1024)S(1)} %fusion.40), kind=kOutput, calls=%fused_computation.115 | convolution fusion | flops 2417491968 | bytes 11800576 | tf_op jit(solution)/shard_map/dot_general | solution.py:43
  146.1 55.7 %mixer_backward.1 = (bf16[1024,3456]{1,0:T(8,128)(2,1)}, f32[8,1792]{1,0:T(8,128)}, f32[8,128]{1,0:T(8,128)}, f32[8,1536]{1,0:T(8,128)}) custom-call(f32[1024,3456]{1,0:T(8,128)} %fusion.46.proj_ref, f32[1024,1536]{1,0:T(8,128)} %fusion.44.dmix_ref, f32[1024,1536]{1,0:T(8,128)} %get-tuple-element.20.y_ref, f32[8,128,1536]{2,1,0:T(8,128)} %get-tuple-element.21.states_ref, ...), custom_call_target="tpu_custom_call" | custom-call | tf_op jit(solution)/shard_map/mixer_backward/pallas_call | solution.py:335
  201.8 11.8 %fusion.45 = f32[768,3456]{1,0:T(8,128)} fusion(bf16[1024,3456]{1,0:T(8,128)(2,1)} %get-tuple-element.23, f32[1024,768]{1,0:T(8,128)S(1)} %copy-done, f32[768]{0:T(1024)S(1)} %slice.79, f32[1024]{0:T(1024)S(1)} %fusion.42), kind=kOutput, calls=%fused_computation.116 | convolution fusion | flops 5438177280 | bytes 20847616 | tf_op jit(solution)/shard_map/dot_general | solution.py:43
  213.7 35.9 %reduce-scatter.5.cloned.1.call-done = f32[48,768]{1,0:T(8,128)} async-done(((f32[1536,768]{1,0:T(8,128)}), f32[48,768]{1,0:T(8,128)}) %reduce-scatter.5.cloned.1.call-update) | async-done | bytes 147472 | tf_op jit(solution)/shard_map/reduce_scatter | solution.py:439
  249.9 147.7 %reduce-scatter.7.cloned.1.call-done = f32[24,3456]{1,0:T(8,128)} async-done(((f32[768,3456]{1,0:T(8,128)}), f32[24,3456]{1,0:T(8,128)}) %reduce-scatter.7.cloned.1.call-update) | async-done | bytes 331792
  397.6 0.9 slice_reduce_fusion.1
  399.5 11.1 %multiply_reduce_fusion = (f32[768]{0:T(1024)S(1)}, f32[1024]{0:T(1024)S(1)}, f32[1024,768]{1,0:T(8,128)}) fusion(f32[1024,768]{1,0:T(8,128)S(1)} %copy-done, f32[1024]{0:T(1024)S(1)} %fusion.42, f32[768]{0:T(1024)S(1)} %slice.79, bf16[1024,3456]{1,0:T(8,128)(2,1)} %get-tuple-element.23, bf16[768,3456]{1,0:T(8,128)(2,1)} %all-gather.5.cloned.1.call-done), kind=kOutput, calls=%fused_computation.3 | convolution fusion | flops 5440534528 | bytes 18692096 | tf_op jit(solution)/shard_map/dot_general | solution.py:43
  410.7 40.3 %psum.7 = f32[12288]{0:T(1024)S(1)} all-reduce(f32[12288]{0:T(1024)S(1)} %pad.24), channel_id=1, replica_groups=mesh['rep'=8,'shard'=4] {'rep','shard'}, use_global_device_ids=true, to_apply=%region_16.17 | all-reduce | flops 12288 | bytes 98304 | tf_op jit(solution)/shard_map/psum | solution.py:511
  451.7 5.4 %fusion = f32[1024,768]{1,0:T(8,128)} fusion(f32[1024,768]{1,0:T(8,128)} %param.13, f32[1024,768]{1,0:T(8,128)S(1)} %copy-done, f32[1024,768]{1,0:T(8,128)} %get-tuple-element.62, f32[1024]{0:T(1024)S(1)} %multiply_multiply_fusion.3, f32[768]{0:T(1024)S(1)} %slice.79, f32[1024]{0:T(1024)S(1)} %fusion.42), kind=kLoop, calls=%fused_computation.2 | loop fusion | flops 4718592 | bytes 12594176 | tf_op jit(solution)/shard_map/add | solution.py:497
  457.1 4.3 multiply_add_fusion
  461.4 4.8 %multiply_subtract_fusion.1 = (f32[384,768]{1,0:T(8,128)}, f32[384,768]{1,0:T(8,128)}, f32[384,768]{1,0:T(8,128)}) fusion(f32[384,768]{1,0:T(8,128)} %param.18, f32[384,768]{1,0:T(8,128)} %all-gather.11.cloned.1.call-done, f32[384,768]{1,0:T(8,128)} %param.19, f32[384,768]{1,0:T(8,128)} %param.20), kind=kLoop, calls=%fused_computation.16 | loop fusion | flops 4423680 | bytes 8257536 | tf_op jit(solution)/shard_map/sub | solution.py:432
  466.3 7.8 %multiply_subtract_fusion = (f32[192,3352]{1,0:T(8,128)}, f32[192,3352]{1,0:T(8,128)}, f32[192,3352]{1,0:T(8,128)}) fusion(f32[192,3352]{1,0:T(8,128)S(1)} %copy-done.1, f32[192,3456]{1,0:T(8,128)} %all-gather.9.cloned.1.call-done, f32[192,3352]{1,0:T(8,128)} %param.16, f32[192,3352]{1,0:T(8,128)} %param.17), kind=kLoop, calls=%fused_computation.10 | loop fusion | flops 9653760 | bytes 18020352 | tf_op jit(solution)/shard_map/sub | solution.py:432
  (90 shorter events, 14.2 us)
Async XLA Ops:
  7.2 72.0 %all-gather.5.cloned.1.call-start = ((), (), s32[]{:S(2)}) async-start(), calls=%async_computation.2 | async-start | bytes 5474304 | tf_op jit(solution)/shard_map/all_gather | solution.py:446
  8.1 4.4 copy-start.13
  10.8 127.5 %all-gather.7.cloned.1.call-start = ((), (), s32[]{:S(2)}) async-start(), calls=%async_computation.3 | async-start | bytes 2433024 | tf_op jit(solution)/shard_map/all_gather | solution.py:446
  12.4 237.2 %reduce-scatter.5.cloned.1.call-start = ((), (), s32[]{:S(2)}) async-start(), calls=%async_computation.5 | async-start | bytes 4866048 | tf_op jit(solution)/shard_map/reduce_scatter | solution.py:439
  13.4 8.2 %copy-start.5 = (s32[1024]{0:T(1024)}, s32[1024]{0:T(1024)S(1)}, u32[]{:S(2)}) copy-start(s32[1024]{0:T(1024)S(1)} %get-tuple-element.32) | copy-start | bytes 12292
  22.7 12.0 %copy-start = (f32[1024,768]{1,0:T(8,128)S(1)}, f32[1024,768]{1,0:T(8,128)}, u32[]{:S(2)}) copy-start(f32[1024,768]{1,0:T(8,128)} %param.12) | copy-start | bytes 9437188
  28.3 6.6 %copy-start.6 = (s32[1024]{0:T(1024)S(1)}, s32[1024]{0:T(1024)}, u32[]{:S(2)}) copy-start(s32[1024]{0:T(1024)} %copy-done.5) | copy-start | bytes 12292
  33.2 2.4 copy-start.2
  84.0 11.7 %copy-start.10 = (f32[8]{0:T(128)S(1)}, f32[8]{0:T(128)}, u32[]{:S(2)}) copy-start(f32[8]{0:T(128)} %slice.63) | copy-start | bytes 100
  96.4 21.3 %copy-start.3 = (f32[1024,768]{1,0:T(8,128)S(1)}, f32[1024,768]{1,0:T(8,128)}, u32[]{:S(2)}) copy-start(f32[1024,768]{1,0:T(8,128)} %param.13) | copy-start | bytes 9437188
  124.5 273.1 %reduce-scatter.7.cloned.1.call-start = ((), (), s32[]{:S(2)}) async-start(), calls=%async_computation.7 | async-start | bytes 10948608
  213.6 184.0 %copy-start.7 = (f32[8,1792]{1,0:T(8,128)S(1)}, f32[8,1792]{1,0:T(8,128)}, u32[]{:S(2)}) copy-start(f32[8,1792]{1,0:T(8,128)} %get-tuple-element.24) | copy-start | bytes 172036
  213.6 247.8 %all-gather.11.cloned.1.call-start = ((), (), s32[]{:S(2)}) async-start(), calls=%async_computation.6 | async-start | bytes 1327104 | tf_op jit(solution)/shard_map/all_gather | solution.py:440
  249.6 216.6 %all-gather.9.cloned.1.call-start = ((), (), s32[]{:S(2)}) async-start(), calls=%async_computation.4 | async-start | bytes 2985984 | tf_op jit(solution)/shard_map/all_gather | solution.py:440
  399.5 51.4 %copy-start.4 = (f32[2834]{0:T(1024)S(1)}, f32[2834]{0:T(1024)}, u32[]{:S(2)}) copy-start(f32[2834]{0:T(1024)} %param.21) | copy-start | bytes 34012
  399.5 51.4 %copy-start.8 = (f32[2834]{0:T(1024)S(1)}, f32[2834]{0:T(1024)}, u32[]{:S(2)}) copy-start(f32[2834]{0:T(1024)} %param.22) | copy-start | bytes 34012
  399.5 51.5 %copy-start.9 = (f32[2834]{0:T(1024)S(1)}, f32[2834]{0:T(1024)}, u32[]{:S(2)}) copy-start(f32[2834]{0:T(1024)} %param.23) | copy-start | bytes 34012
  451.7 5.4 %copy-start.11 = (bf16[1024,1536]{1,0:T(8,128)(2,1)S(1)}, bf16[1024,1536]{1,0:T(8,128)(2,1)}, u32[]{:S(2)}) copy-start(bf16[1024,1536]{1,0:T(8,128)(2,1)} %get-tuple-element.19) | copy-start | bytes 9437188
  451.7 5.4 %copy-start.12 = (bf16[1536,768]{1,0:T(8,128)(2,1)S(1)}, bf16[1536,768]{1,0:T(8,128)(2,1)}, u32[]{:S(2)}) copy-start(bf16[1536,768]{1,0:T(8,128)(2,1)} %all-gather.7.cloned.1.call-done) | copy-start | bytes 7077892
  461.4 4.8 %copy-start.1 = (f32[192,3352]{1,0:T(8,128)S(1)}, f32[192,3352]{1,0:T(8,128)}, u32[]{:S(2)}) copy-start(f32[192,3352]{1,0:T(8,128)} %param.15) | copy-start | bytes 7723012
Sparse Core Ops, SparseCore 0:
  10.9 68.2 all-gather.4
  82.1 56.1 all-gather.6
  143.7 105.8 reduce-scatter.4
  256.6 140.9 reduce-scatter.6
  399.5 23.3 all-gather.10
  424.8 30.6 all-gather.8
